TPU v7x, 1024 devices: a whole 4x4x32 slice. The times are simulated.
1024 devices in a mesh: ax: 256 (over z_lo, y, x, core), az: 4 (over z_hi).
Axes of the slice: x: 4, y: 4, z: 32 (z_hi: 4, z_lo: 8; z = z_hi * 8 + z_lo), core: 2. Of those that a mesh axis runs over, the one named last changes fastest.
Arguments:
- conserved: float32 [1024, 5, 32, 512], P('ax', None, None, 'az'), may hold values from -1.1 to 6.2, as said below
- cycle_modes: int32 [32], replicated, may hold values from 1 to 64, as said below
- filtered_cycles: int32 [1024], P('ax'), may hold values from 1 to 32, as said below
Outputs:
- stepped: float32 [1024, 5, 32, 512], P('ax', None, None, 'az')
Inputs may be any that keep to these rules, and one draw needn't show every extreme that they name: `conserved`: density is at least 0.3 and pressure at least 0.02 in every cell. `cycle_modes`: 64 and 1 both occur. `filtered_cycles`: 32 and 1 both occur.
All inputs are finite; a program needn't handle non-finite values.
Results may differ from a plain program's by a relative error of at most 0.0003.
Values sent between devices are 32-bit elements; how exact they have to be, the bound alone decides.
A program may use at most 32 MiB of HBM per device.

v0:
```python
import math

import jax
import jax.numpy as jnp
from jax import lax
from jax.sharding import PartitionSpec as P

NT = 512
NRF = 32
MODE_MOST = 64


STENCIL = (0.8, -0.2, 4.0 / 105.0, -1.0 / 280.0)
GAS_FACTOR = 0.4
TIME_STEP = 0.1


def extended(cells, sides, width, closed):
    for axis, dim in sides:
        count = lax.axis_size(axis)
        ends = count if closed else count - 1
        head = lax.slice_in_dim(cells, 0, width, axis=dim)
        tail = lax.slice_in_dim(cells, cells.shape[dim] - width, cells.shape[dim], axis=dim)
        cells = jnp.concatenate(
            [
                lax.ppermute(tail, axis, [(i, (i + 1) % count) for i in range(ends)]),
                cells,
                lax.ppermute(head, axis, [((i + 1) % count, i) for i in range(ends)]),
            ],
            axis=dim,
        )
    return cells


def partner(block, axis, distance):
    count = lax.axis_size(axis)
    route = []
    for low in range(count):
        high = low | 1 << distance
        if high != low and high < count:
            route += [(low, high), (high, low)]
    return lax.ppermute(block, axis, route)


def velocities(fields):
    density = fields[:, 0]
    axial_vel = fields[:, 1] / density
    radial_vel = fields[:, 2] / density
    swirl_vel = fields[:, 3] / density
    kinetic = fields[:, 1] * axial_vel + fields[:, 2] * radial_vel + fields[:, 3] * swirl_vel
    pressure = GAS_FACTOR * (fields[:, 4] - 0.5 * kinetic)
    return (axial_vel, radial_vel, swirl_vel, pressure)


def axial_flux(fields):
    axial_vel, radial_vel, swirl_vel, pressure = velocities(fields)
    return jnp.stack(
        [
            fields[:, 1],
            fields[:, 1] * axial_vel + pressure,
            fields[:, 2] * axial_vel,
            fields[:, 3] * axial_vel,
            axial_vel * (fields[:, 4] + pressure),
        ],
        axis=1,
    )


def radial_flux(fields):
    axial_vel, radial_vel, swirl_vel, pressure = velocities(fields)
    return jnp.stack(
        [
            fields[:, 2],
            fields[:, 1] * radial_vel,
            fields[:, 2] * radial_vel + pressure,
            fields[:, 3] * radial_vel,
            radial_vel * (fields[:, 4] + pressure),
        ],
        axis=1,
    )


def swirl_flux(fields):
    axial_vel, radial_vel, swirl_vel, pressure = velocities(fields)
    return jnp.stack(
        [
            fields[:, 3],
            fields[:, 1] * swirl_vel,
            fields[:, 2] * swirl_vel,
            fields[:, 3] * swirl_vel + pressure,
            swirl_vel * (fields[:, 4] + pressure),
        ],
        axis=1,
    )


def central_difference(values, along, extent):
    result = None
    for offset, weight in zip((1, 2, 3, 4), STENCIL):
        forward_part = lax.slice_in_dim(values, 4 + offset, 4 + offset + extent, axis=along)
        backward_part = lax.slice_in_dim(values, 4 - offset, 4 - offset + extent, axis=along)
        contribution = weight * (forward_part - backward_part)
        result = contribution if result is None else result + contribution
    return result


def section_update(axial_padded, theta_padded, opposite, fields):
    stations = fields.shape[0]
    radial = fields.shape[2]
    width = fields.shape[3]
    axial_term = central_difference(axial_flux(axial_padded), 0, stations)
    flips = jnp.array([1.0, 1.0, -1.0, -1.0, 1.0], jnp.float32).reshape(1, 5, 1, 1)
    mirrored = opposite[:, :, ::-1, :] * flips
    outer_rows = jnp.broadcast_to(fields[:, :, -1:, :], (stations, 5, 4, width))
    radial_padded = jnp.concatenate([mirrored, fields, outer_rows], axis=2)
    signed_radius = (jnp.arange(radial + 8, dtype=jnp.float32) - 3.5).reshape(1, 1, -1, 1)
    radial_term = central_difference(radial_flux(radial_padded) * signed_radius, 2, radial)
    swirl_term = central_difference(swirl_flux(theta_padded), 3, width) * (NT / (2.0 * math.pi))
    axial_vel, radial_vel, swirl_vel, pressure = velocities(fields)
    nothing = jnp.zeros_like(pressure)
    source = jnp.stack(
        [nothing, nothing, fields[:, 3] * swirl_vel + pressure, -fields[:, 2] * swirl_vel, nothing],
        axis=1,
    )
    radius = (jnp.arange(radial, dtype=jnp.float32) + 0.5).reshape(1, 1, -1, 1)
    tendency = -axial_term - (radial_term + swirl_term - source) / radius
    return fields + TIME_STEP * tendency


def fourier_basis(columns):
    harmonic = jnp.arange(2 * MODE_MOST, dtype=jnp.int32) % MODE_MOST
    product = columns[:, None] * harmonic[None, :] % NT
    angle = product.astype(jnp.float32) * (2.0 * math.pi / NT)
    cosine_side = (jnp.arange(2 * MODE_MOST, dtype=jnp.int32) < MODE_MOST)[None, :]
    return jnp.where(cosine_side, jnp.cos(angle), jnp.sin(angle))


def mode_weights(cycle_modes):
    harmonic = jnp.arange(2 * MODE_MOST, dtype=jnp.int32) % MODE_MOST
    base_weight = jnp.where(harmonic == 0, 1.0 / NT, 2.0 / NT).astype(jnp.float32)
    keep = harmonic[None, :] < cycle_modes[:, None]
    return jnp.where(keep, base_weight[None, :], 0.0)


def per_device(conserved, cycle_modes, filtered_cycles):
    axial_padded = extended(conserved, (("ax", 0),), 4, False)
    theta_padded = extended(conserved, (("az", 3),), 4, True)
    position = lax.axis_index("ax")
    last_index = lax.axis_size("ax") - 1
    low_edge = jnp.broadcast_to(conserved[:1], (4,) + conserved.shape[1:])
    high_edge = jnp.broadcast_to(conserved[-1:], (4,) + conserved.shape[1:])
    axial_padded = jnp.concatenate(
        [
            jnp.where(position == 0, low_edge, axial_padded[:4]),
            axial_padded[4:-4],
            jnp.where(position == last_index, high_edge, axial_padded[-4:]),
        ],
        axis=0,
    )
    partner_bit = lax.axis_size("az").bit_length() - 2
    opposite = partner(conserved[:, :, :4, :], "az", partner_bit)
    section = section_update(axial_padded, theta_padded, opposite, conserved)
    kept_weights = mode_weights(cycle_modes)
    sector = lax.axis_index("az")
    per_sector = NRF // lax.axis_size("az")
    lines = lax.all_to_all(section, "az", split_axis=2, concat_axis=3, tiled=True)
    full_basis = fourier_basis(jnp.arange(NT, dtype=jnp.int32))
    local_weights = lax.dynamic_slice_in_dim(kept_weights, sector * per_sector, per_sector, 0)
    coefficients = jnp.einsum("afrt,tc->afrc", lines, full_basis, precision=lax.Precision.HIGHEST)
    smoothed = jnp.einsum(
        "afrc,tc->afrt",
        coefficients * local_weights[None, None],
        full_basis,
        precision=lax.Precision.HIGHEST,
    )
    local_ids = sector * per_sector + jnp.arange(per_sector, dtype=jnp.int32)
    chosen = jnp.where(
        local_ids[None, None, :, None] < filtered_cycles[:, None, None, None], smoothed, lines
    )
    result_cycles = lax.all_to_all(chosen, "az", split_axis=3, concat_axis=2, tiled=True)
    return jnp.concatenate([result_cycles, section[:, :, NRF:, :]], axis=2)


def solution(mesh):
    placed = (P("ax", None, None, "az"), P(), P("ax"))
    return jax.shard_map(
        per_device, mesh=mesh, in_specs=placed, out_specs=P("ax", None, None, "az"), check_vma=False
    )
```

profile of v0, /device:TPU:39, one launch (start us, length us, event | category | flops | bytes accessed | tf_op | source)
XLA Modules:
  0.0 243.6 jit_solution(1759651708081721562)
XLA Ops:
  0.0 2.7 %collective-permute-start.1 = (f32[4,5,32,128]{3,2,1,0:T(8,128)}, f32[4,5,32,128]{3,2,1,0:T(8,128)S(1)}, u32[]{:S(2)}, u32[]{:S(2)}) collective-permute-start(f32[4,5,32,128]{3,2,1,0:T(8,128)} %param.4), channel_id=1, source_target_pairs={{4,0},{8,4},{12,8},{16,12},{20,16},{24,20},{28,24},{32,28},{36,32}... | collective-permute-start | bytes 983048 | tf_op jit(solution)/shard_map/ppermute | solution.py:28
  2.7 5.1 %collective-permute-start = (f32[4,5,32,128]{3,2,1,0:T(8,128)}, f32[4,5,32,128]{3,2,1,0:T(8,128)S(1)}, u32[]{:S(2)}, u32[]{:S(2)}) collective-permute-start(f32[4,5,32,128]{3,2,1,0:T(8,128)} %param.4), channel_id=1, source_target_pairs={{0,4},{4,8},{8,12},{12,16},{16,20},{20,24},{24,28},{28,32},{32,36}... | collective-permute-start | bytes 983048 | tf_op jit(solution)/shard_map/ppermute | solution.py:26
  7.8 1.2 fusion.69
  9.1 15.4 %collective-permute-start.3 = (f32[4,5,32,4]{3,2,1,0:T(8,128)S(1)}, f32[4,5,32,4]{3,2,1,0:T(8,128)S(1)}, u32[]{:S(2)}, u32[]{:S(2)}) collective-permute-start(f32[4,5,32,4]{3,2,1,0:T(8,128)S(1)} %get-tuple-element.18), channel_id=1, source_target_pairs={{0,1},{1,2},{2,3},{3,0},{4,5},{5,6},{6,7},{7,4},{8,9},{9,10},{10,1... | collective-permute-start | bytes 30728 | tf_op jit(solution)/shard_map/ppermute | solution.py:26
  24.5 8.3 %collective-permute-start.4 = (f32[4,5,32,4]{3,2,1,0:T(8,128)S(1)}, f32[4,5,32,4]{3,2,1,0:T(8,128)S(1)}, u32[]{:S(2)}, u32[]{:S(2)}) collective-permute-start(f32[4,5,32,4]{3,2,1,0:T(8,128)S(1)} %get-tuple-element.19), channel_id=1, source_target_pairs={{1,0},{2,1},{3,2},{0,3},{5,4},{6,5},{7,6},{4,7},{9,8},{10,9},{11,1... | collective-permute-start | bytes 30728 | tf_op jit(solution)/shard_map/ppermute | solution.py:28
  33.7 18.0 %collective-permute-start.2 = (f32[4,5,4,128]{3,2,1,0:T(4,128)S(1)}, f32[4,5,4,128]{3,2,1,0:T(4,128)S(1)}, u32[]{:S(2)}, u32[]{:S(2)}) collective-permute-start(f32[4,5,4,128]{3,2,1,0:T(4,128)S(1)} %slice.194), channel_id=1, source_target_pairs={{0,2},{2,0},{1,3},{3,1},{4,6},{6,4},{5,7},{7,5},{8,10},{10,8},{9,1... | collective-permute-start | bytes 122888 | tf_op jit(solution)/shard_map/ppermute | solution.py:42
  51.8 0.9 slice_bitcast_fusion.1
  52.7 1.0 fusion.57
  53.8 0.9 slice.195
  54.8 7.7 %collective-permute-done.3 = f32[4,5,32,4]{3,2,1,0:T(8,128)S(1)} collective-permute-done((f32[4,5,32,4]{3,2,1,0:T(8,128)S(1)}, f32[4,5,32,4]{3,2,1,0:T(8,128)S(1)}, u32[]{:S(2)}, u32[]{:S(2)}) %collective-permute-start.3) | collective-permute-done | bytes 10272 | tf_op jit(solution)/shard_map/ppermute | solution.py:26
  62.5 31.9 %collective-permute-done.4 = f32[4,5,32,4]{3,2,1,0:T(8,128)S(1)} collective-permute-done((f32[4,5,32,4]{3,2,1,0:T(8,128)S(1)}, f32[4,5,32,4]{3,2,1,0:T(8,128)S(1)}, u32[]{:S(2)}, u32[]{:S(2)}) %collective-permute-start.4) | collective-permute-done | bytes 10272 | tf_op jit(solution)/shard_map/ppermute | solution.py:28
  94.4 1.3 pad_maximum_fusion.1
  95.9 10.2 %collective-permute-done.2 = f32[4,5,4,128]{3,2,1,0:T(4,128)S(1)} collective-permute-done((f32[4,5,4,128]{3,2,1,0:T(4,128)S(1)}, f32[4,5,4,128]{3,2,1,0:T(4,128)S(1)}, u32[]{:S(2)}, u32[]{:S(2)}) %collective-permute-start.2) | collective-permute-done | bytes 40992 | tf_op jit(solution)/shard_map/ppermute | solution.py:42
  107.7 1.0 copy.51
  108.7 10.3 %all-to-all-start = ((f32[4,5,32,128]{3,1,0,2:T(8,128)}), f32[4,5,32,128]{3,1,0,2:T(8,128)S(1)}, u32[]{:S(2)}, u32[]{:S(2)}) async-start(f32[4,5,32,128]{3,1,0,2:T(8,128)} %copy.51), calls=%async_computation | async-start | bytes 1048576 | tf_op jit(solution)/shard_map/all_to_all | solution.py:166
  119.3 48.3 %all-to-all-done = f32[4,5,32,128]{3,1,0,2:T(8,128)S(1)} async-done(((f32[4,5,32,128]{3,1,0,2:T(8,128)}), f32[4,5,32,128]{3,1,0,2:T(8,128)S(1)}, u32[]{:S(2)}, u32[]{:S(2)}) %all-to-all-start) | async-done | bytes 327712 | tf_op jit(solution)/shard_map/all_to_all | solution.py:166
  167.6 1.5 convolution_multiply_fusion
  169.2 1.6 convolution_select_fusion
  170.8 3.5 %copy.53 = f32[4,5,8,512]{2,0,1,3:T(4,128)} copy(f32[4,5,8,512]{3,2,1,0:T(8,128)S(1)} %convolution_select_fusion) | data formatting | bytes 655360 | tf_op jit(solution)/shard_map/jit(_where)/select_n | solution.py:177
  174.3 7.8 %reshape.69 = f32[4,1,20480]{2,1,0:T(1,128)S(1)} reshape(f32[512,5,4,8]{3,2,1,0:T(4,128)} %bitcast.29) | data formatting | bytes 655360
  182.0 46.1 %all_to_all.36 = f32[4,1,20480]{2,1,0:T(1,128)S(1)} all-to-all(f32[4,1,20480]{2,1,0:T(1,128)S(1)} %reshape.69), channel_id=1, replica_groups=mesh['ax'=256,'az'=4] {'az'}, dimensions={0} | all-to-all | bytes 655360 | tf_op jit(solution)/shard_map/all_to_all | solution.py:180
  228.6 1.6 reduce
  230.2 8.7 %reshape.70 = f32[512,5,4,8]{3,2,1,0:T(4,128)} reshape(f32[4,20480]{1,0:T(4,128)S(1)} %reduce) | data formatting | bytes 655360
  238.8 4.7 %copy.54 = f32[4,5,4,8,128]{4,3,2,1,0:T(8,128)} copy(f32[4,5,4,8,128]{3,0,1,4,2:T(4,128)} %bitcast.30) | data formatting | bytes 655360 | tf_op jit(solution)/shard_map/all_to_all | solution.py:180
  (50 shorter events, 3.4 us)
Async XLA Ops:
  0.0 106.2 %copy-start.1 = (f32[5]{0:T(128)S(1)}, f32[5]{0:T(128)}, u32[]{:S(2)}) copy-start(f32[5]{0:T(128)} %constant.89.clone) | copy-start | bytes 64
  0.0 106.3 %copy-start = (f32[4,5,32,128]{3,2,1,0:T(8,128)S(1)}, f32[4,5,32,128]{3,2,1,0:T(8,128)}, u32[]{:S(2)}) copy-start(f32[4,5,32,128]{3,2,1,0:T(8,128)} %param.4) | copy-start | bytes 983044
  0.0 106.6 %collective-permute-start.1 = (f32[4,5,32,128]{3,2,1,0:T(8,128)}, f32[4,5,32,128]{3,2,1,0:T(8,128)S(1)}, u32[]{:S(2)}, u32[]{:S(2)}) collective-permute-start(f32[4,5,32,128]{3,2,1,0:T(8,128)} %param.4), channel_id=1, source_target_pairs={{4,0},{8,4},{12,8},{16,12},{20,16},{24,20},{28,24},{32,28},{36,32}... | collective-permute-start | bytes 983048 | tf_op jit(solution)/shard_map/ppermute | solution.py:28
  2.7 103.9 %collective-permute-start = (f32[4,5,32,128]{3,2,1,0:T(8,128)}, f32[4,5,32,128]{3,2,1,0:T(8,128)S(1)}, u32[]{:S(2)}, u32[]{:S(2)}) collective-permute-start(f32[4,5,32,128]{3,2,1,0:T(8,128)} %param.4), channel_id=1, source_target_pairs={{0,4},{4,8},{8,12},{12,16},{16,20},{20,24},{24,28},{28,32},{32,36}... | collective-permute-start | bytes 983048 | tf_op jit(solution)/shard_map/ppermute | solution.py:26
  9.1 53.4 %collective-permute-start.3 = (f32[4,5,32,4]{3,2,1,0:T(8,128)S(1)}, f32[4,5,32,4]{3,2,1,0:T(8,128)S(1)}, u32[]{:S(2)}, u32[]{:S(2)}) collective-permute-start(f32[4,5,32,4]{3,2,1,0:T(8,128)S(1)} %get-tuple-element.18), channel_id=1, source_target_pairs={{0,1},{1,2},{2,3},{3,0},{4,5},{5,6},{6,7},{7,4},{8,9},{9,10},{10,1... | collective-permute-start | bytes 30728 | tf_op jit(solution)/shard_map/ppermute | solution.py:26
  24.5 69.9 %collective-permute-start.4 = (f32[4,5,32,4]{3,2,1,0:T(8,128)S(1)}, f32[4,5,32,4]{3,2,1,0:T(8,128)S(1)}, u32[]{:S(2)}, u32[]{:S(2)}) collective-permute-start(f32[4,5,32,4]{3,2,1,0:T(8,128)S(1)} %get-tuple-element.19), channel_id=1, source_target_pairs={{1,0},{2,1},{3,2},{0,3},{5,4},{6,5},{7,6},{4,7},{9,8},{10,9},{11,1... | collective-permute-start | bytes 30728 | tf_op jit(solution)/shard_map/ppermute | solution.py:28
  33.7 72.4 %collective-permute-start.2 = (f32[4,5,4,128]{3,2,1,0:T(4,128)S(1)}, f32[4,5,4,128]{3,2,1,0:T(4,128)S(1)}, u32[]{:S(2)}, u32[]{:S(2)}) collective-permute-start(f32[4,5,4,128]{3,2,1,0:T(4,128)S(1)} %slice.194), channel_id=1, source_target_pairs={{0,2},{2,0},{1,3},{3,1},{4,6},{6,4},{5,7},{7,5},{8,10},{10,8},{9,1... | collective-permute-start | bytes 122888 | tf_op jit(solution)/shard_map/ppermute | solution.py:42
  107.0 12.1 %copy-start.2 = (s32[32]{0:T(128)S(1)}, s32[32]{0:T(128)}, u32[]{:S(2)}) copy-start(s32[32]{0:T(128)} %param.5) | copy-start | bytes 388
  107.0 12.2 %copy-start.3 = (s32[4]{0:T(128)S(1)}, s32[4]{0:T(128)}, u32[]{:S(2)}) copy-start(s32[4]{0:T(128)} %param.6) | copy-start | bytes 52
  108.7 58.9 %all-to-all-start = ((f32[4,5,32,128]{3,1,0,2:T(8,128)}), f32[4,5,32,128]{3,1,0,2:T(8,128)S(1)}, u32[]{:S(2)}, u32[]{:S(2)}) async-start(f32[4,5,32,128]{3,1,0,2:T(8,128)} %copy.51), calls=%async_computation | async-start | bytes 1048576 | tf_op jit(solution)/shard_map/all_to_all | solution.py:166
where the time goes:
time: 244 us
  waiting for transfers between devices  98.1 us (40%)
  starting transfers between devices  59.9 us (25%)
  blocking collectives  46.1 us (19%)
  local copies, waits for them, and re-layouts  30.4 us (12%)
  other arithmetic  5.57 us (2%)
  matrix products  3.13 us (1%)
    all_to_all x1, waiting for transfers between devices, per_device(): lax.all_to_all(section, 'az', split_axis=2, concat_axis=3, tiled=True)  48.3 us
    all_to_all x1, blocking collectives, per_device(): lax.all_to_all(chosen, 'az', split_axis=3, concat_axis=2, tiled=True)  46.1 us
    ppermute x2, waiting for transfers between devices, extended(): lax.ppermute(head, axis, [((i + 1) % count, i) for i in range(ends)])  31.9 us
    ppermute x2, starting transfers between devices, extended(): lax.ppermute(tail, axis, [(i, (i + 1) % count) for i in range(ends)])  20.5 us
    ppermute x1, starting transfers between devices, partner(): return lax.ppermute(block, axis, route)  18 us
    unnamed x13, local copies, waits for them, and re-layouts  16.5 us
    ppermute x2, starting transfers between devices, extended(): lax.ppermute(head, axis, [((i + 1) % count, i) for i in range(ends)])  11 us
    all_to_all x1, starting transfers between devices, per_device(): lax.all_to_all(section, 'az', split_axis=2, concat_axis=3, tiled=True)  10.3 us
  transfers between devices with their start and end apart: 6, of which 4 were waited for; matrix products, arithmetic and copies ran while one was open for 3% of the time, Pallas kernels for 0%

commit v1 on v0

v1 whole, which is shorter than its diff:
```python
import functools
import math

import jax
import jax.numpy as jnp
import numpy as np
from jax import lax
from jax.experimental import pallas as pl
from jax.experimental.pallas import tpu as pltpu
from jax.sharding import PartitionSpec as P

NT = 512
NRF = 32
MODE_MOST = 64
STENCIL = (0.8, -0.2, 4.0 / 105.0, -1.0 / 280.0)
GAS_FACTOR = 0.4
TIME_STEP = 0.1

SECTORS = 4
WIDTH = NT // SECTORS
STATIONS = 4
FIELDS = 5
ROWS = 32
LINES = STATIONS * ROWS
NEAR = 12
FAR = 6
MESH = pl.DeviceIdType.MESH
EXACT = lax.Precision.HIGHEST
MIRROR_SIGNS = (1.0, 1.0, -1.0, -1.0, 1.0)


def kernel_factors(distance, rank):
    cells = np.arange(WIDTH)
    gap = WIDTH * distance + cells[:, None] - cells[None, :]
    left, values, right = np.linalg.svd(1.0 / np.sin(np.pi * gap / NT))
    root = np.sqrt(values[:rank])
    return (left[:, :rank] * root).T, right[:rank] * root[:, None]


def build_tables():
    parts = {}
    radius = np.arange(ROWS) + 0.5
    ring = np.zeros((ROWS, ROWS))
    mirror = np.zeros((4, ROWS))
    for row in range(ROWS):
        for k, weight in enumerate(STENCIL, 1):
            ring[row, min(row + k, ROWS - 1)] -= TIME_STEP * weight * (row + k + 0.5) / radius[row]
            below = row - k
            if below >= 0:
                ring[row, below] += TIME_STEP * weight * (below + 0.5) / radius[row]
            else:
                mirror[row, -1 - below] += TIME_STEP * weight * (-below - 0.5) / radius[row]
    parts["radial"] = np.kron(np.eye(STATIONS), ring)
    parts["mirror"] = np.kron(np.eye(STATIONS), mirror)
    swirl = np.zeros((WIDTH, WIDTH))
    edge = np.zeros((8, WIDTH))
    place = np.zeros((8, WIDTH))
    for cell in range(-4, WIDTH + 4):
        for k, weight in enumerate(STENCIL, 1):
            for source, value in ((cell + k, -weight), (cell - k, weight)):
                if 0 <= source < WIDTH:
                    if cell < 0:
                        edge[cell + 4, source] += value
                    elif cell >= WIDTH:
                        edge[cell - WIDTH + 4, source] += value
                    else:
                        swirl[source, cell] += value
    for cell in range(4):
        place[cell, WIDTH - 4 + cell] = 1.0
        place[4 + cell, cell] = 1.0
    parts["swirl"] = swirl
    parts["edge"] = edge
    parts["place"] = place
    angle = 2.0 * np.pi / NT * np.arange(WIDTH)[:, None] * np.arange(MODE_MOST)[None, :]
    parts["basis"] = np.concatenate([np.cos(angle), np.sin(angle)], axis=1)
    source_a = np.zeros((64, WIDTH))
    source_b = np.zeros((64, WIDTH))
    target_a = np.zeros((64, WIDTH))
    target_b = np.zeros((64, WIDTH))
    first = 0
    for distance, rank in ((1, NEAR), (-1, NEAR), (2, FAR)):
        target, source = kernel_factors(distance, rank)
        source_a[first : first + rank] = source
        source_b[first + rank : first + 2 * rank] = source
        target_a[first : first + rank] = target / NT
        target_b[first + rank : first + 2 * rank] = -target / NT
        first += 2 * rank
    parts["source_a"] = source_a
    parts["source_b"] = source_b
    parts["target_a"] = target_a
    parts["target_b"] = target_b
    spans, blocks, start = {}, [], 0
    for name, block in parts.items():
        spans[name] = (start, start + block.shape[0])
        start += block.shape[0]
        blocks.append(block)
    return np.concatenate(blocks, axis=0).astype(np.float32), spans


TABLES, SPANS = build_tables()
NEAR_ROWS = 2 * NEAR
FAR_ROWS = 2 * FAR
MESSAGE_ROWS = 2 * NEAR_ROWS + FAR_ROWS


def matmul(left, right, dims=((1,), (0,))):
    return lax.dot_general(left, right, (dims, ((), ())), precision=EXACT, preferred_element_type=jnp.float32)


def sector_waves(modes, sector):
    cell = lax.broadcasted_iota(jnp.int32, modes.shape, 1) + sector * WIDTH
    turn = ((2 * modes - 1) * cell) & (2 * NT - 1)
    angle = turn.astype(jnp.float32) * (math.pi / NT)
    return jnp.cos(angle), jnp.sin(angle)


def body(
    conserved, tables, modes, counts, out,
    cells, table, flux_f, flux_g, flux_h,
    axial_out, axial_in, edge_out, edge_in, mirror_out, mirror_in, mirror_mod,
    extra_out, extra_in, extra_own, section, modulated, message_out, message_in, compact,
    load_sem, send_sem, recv_sem,
):
    ax = lax.axis_index("ax")
    az = lax.axis_index("az")
    ax_count = lax.axis_size("ax")
    right = lax.rem(az + 1, SECTORS)
    left = lax.rem(az + SECTORS - 1, SECTORS)
    across = lax.rem(az + 2, SECTORS)
    has_low = ax > 0
    has_high = ax < ax_count - 1

    barrier = pltpu.get_barrier_semaphore()
    for sector in (right, left, across):
        pl.semaphore_signal(barrier, inc=1, device_id=(ax, sector), device_id_type=MESH)

    @pl.when(has_low)
    def _():
        pl.semaphore_signal(barrier, inc=1, device_id=(ax - 1, az), device_id_type=MESH)

    @pl.when(has_high)
    def _():
        pl.semaphore_signal(barrier, inc=1, device_id=(ax + 1, az), device_id_type=MESH)

    load_cells = pltpu.make_async_copy(conserved, cells, load_sem.at[0])
    load_table = pltpu.make_async_copy(tables, table, load_sem.at[1])
    load_cells.start()
    load_table.start()

    def tab(name):
        low, high = SPANS[name]
        return table[low:high]

    row = lax.broadcasted_iota(jnp.int32, (8, WIDTH), 0)
    lane = lax.broadcasted_iota(jnp.int32, (8, WIDTH), 1)
    mode_tiles = []
    for tile in range(ROWS // 8):
        value = jnp.zeros((8, WIDTH), jnp.int32)
        for j in range(8):
            value = jnp.where(row == j, modes[tile * 8 + j], value)
        mode_tiles.append(value)
    ring_modes = jnp.concatenate(mode_tiles, axis=0)
    inner_modes = jnp.zeros((8, WIDTH), jnp.int32)
    for j in range(4):
        inner_modes = jnp.where((row & 3) == j, modes[j], inner_modes)
    wave_c, wave_s = sector_waves(ring_modes, az)
    inner_c, inner_s = sector_waves(inner_modes, az)
    across_c, across_s = sector_waves(inner_modes, across)
    harmonic = lane & (MODE_MOST - 1)
    base_weight = jnp.where(harmonic == 0, 1.0 / NT, 2.0 / NT).astype(jnp.float32)
    ring_harmonic = lax.broadcasted_iota(jnp.int32, (ROWS, WIDTH), 1) & (MODE_MOST - 1)
    ring_base = jnp.where(ring_harmonic == 0, 1.0 / NT, 2.0 / NT).astype(jnp.float32)
    ring_weight = jnp.where(ring_harmonic < ring_modes, ring_base, 0.0)
    inner_weight = jnp.where(harmonic < inner_modes, base_weight, 0.0)
    ring_row = lax.broadcasted_iota(jnp.int32, (ROWS, WIDTH), 0)
    per_radius = TIME_STEP / (ring_row.astype(jnp.float32) + 0.5)

    load_cells.wait()
    for x in range(STATIONS):
        s0, s1, s2, s3, s4 = (cells[x, c] for c in range(FIELDS))
        inverse = 1.0 / s0
        a = s1 * inverse
        b = s2 * inverse
        d = s3 * inverse
        p = GAS_FACTOR * (s4 - 0.5 * (s1 * a + s2 * b + s3 * d))
        e = s4 + p
        lines = pl.ds(x * ROWS, ROWS)
        flux_f[x, 0], flux_f[x, 1], flux_f[x, 2], flux_f[x, 3], flux_f[x, 4] = s1, s1 * a + p, s2 * a, s3 * a, a * e
        for c, value in enumerate((s2, s1 * b, s2 * b + p, s3 * b, b * e)):
            flux_g[c, lines] = value
        swirl_two = s2 * d
        swirl_three = s3 * d + p
        for c, value in enumerate((s3, s1 * d, swirl_two, swirl_three, d * e)):
            flux_h[c, lines] = value * (per_radius * (NT / (2.0 * math.pi)))
        for c, value in enumerate((s0, s1, s2 + per_radius * swirl_three, s3 - per_radius * swirl_two, s4)):
            section[c, lines] = value
    for c in range(FIELDS):
        for i in range(STATIONS):
            own = from_low = to_high = to_low = None
            for s in range(STATIONS):
                value = flux_f[s, c]
                if s != i:
                    weight = TIME_STEP * STENCIL[abs(s - i) - 1] * (-1.0 if s > i else 1.0)
                    own = weight * value if own is None else own + weight * value
                if s >= i:
                    term = TIME_STEP * STENCIL[3 + i - s] * value
                    to_high = term if to_high is None else to_high + term
                if s <= i:
                    term = -TIME_STEP * STENCIL[3 + s - i] * value
                    to_low = term if to_low is None else to_low + term
            section[c, pl.ds(i * ROWS, ROWS)] += own
            axial_out[1, i, c] = to_high
            axial_out[0, i, c] = to_low
            edge_weight = TIME_STEP * sum(STENCIL[i:])
            pl.when(jnp.logical_not(has_low))(
                functools.partial(store, axial_in, (0, i, c), edge_weight * flux_f[0, c])
            )
            edge_weight = -TIME_STEP * sum(STENCIL[3 - i :])
            pl.when(jnp.logical_not(has_high))(
                functools.partial(store, axial_in, (1, i, c), edge_weight * flux_f[3, c])
            )

    load_table.wait()
    edges = matmul(tab("edge"), flux_h[...].reshape(FIELDS * LINES, WIDTH), ((1,), (1,)))
    edge_out[0] = edges[0:4]
    edge_out[1] = edges[4:8]

    def remote(source, target, slot, device):
        return pltpu.make_async_remote_copy(
            src_ref=source, dst_ref=target, send_sem=send_sem.at[slot], recv_sem=recv_sem.at[slot],
            device_id=device, device_id_type=MESH,
        )

    pl.semaphore_wait(barrier, 3 + has_low.astype(jnp.int32) + has_high.astype(jnp.int32))
    to_high = remote(axial_out.at[1], axial_in.at[0], 0, (ax + 1, az))
    to_low = remote(axial_out.at[0], axial_in.at[1], 1, (ax - 1, az))
    pl.when(has_high)(to_high.start)
    pl.when(has_low)(to_low.start)
    edge_left = remote(edge_out.at[0], edge_in.at[0], 2, (ax, left))
    edge_right = remote(edge_out.at[1], edge_in.at[1], 3, (ax, right))
    edge_left.start()
    edge_right.start()

    mirror_table = tab("mirror")
    for c in range(FIELDS):
        value = MIRROR_SIGNS[c] * matmul(mirror_table, flux_g[c])
        mirror_out[pl.ds(16 * c, 16)] = value
        for half in range(2):
            lines = pl.ds(16 * c + 8 * half, 8)
            mirror_mod[lines, 0:WIDTH] = value[8 * half : 8 * half + 8] * across_c
            mirror_mod[lines, WIDTH : 2 * WIDTH] = value[8 * half : 8 * half + 8] * across_s
    mirror_mod[80:128] = jnp.zeros((48, 2 * WIDTH), jnp.float32)
    mirror_copy = remote(mirror_out, mirror_in, 4, (ax, across))
    mirror_copy.start()
    sources = jnp.concatenate([tab("source_a"), tab("source_b")], axis=1)
    extra = matmul(sources, mirror_mod[...], ((1,), (1,)))
    extra_out[...] = extra[0 : 2 * NEAR_ROWS]
    extra_own[...] = extra[2 * NEAR_ROWS : 64]
    extra_left = remote(extra_out.at[0:NEAR_ROWS], extra_in.at[0:NEAR_ROWS], 5, (ax, left))
    extra_right = remote(
        extra_out.at[NEAR_ROWS : 2 * NEAR_ROWS], extra_in.at[NEAR_ROWS : 2 * NEAR_ROWS], 6, (ax, right)
    )
    extra_left.start()
    extra_right.start()

    radial_table = tab("radial")
    swirl_table = tab("swirl")
    for c in range(FIELDS):
        section[c] += matmul(radial_table, flux_g[c]) + matmul(flux_h[c], swirl_table)

    pl.when(has_high)(to_low_wait(remote(axial_out.at[1], axial_in.at[1], 1, (ax + 1, az))))
    pl.when(has_low)(to_low_wait(remote(axial_out.at[0], axial_in.at[0], 0, (ax - 1, az))))
    edge_left.wait_recv()
    edge_right.wait_recv()
    edges = jnp.concatenate([edge_in[0], edge_in[1]], axis=0)
    place = tab("place")
    for c in range(FIELDS):
        placed = matmul(edges[:, c * LINES : (c + 1) * LINES], place, ((0,), (0,)))
        for x in range(STATIONS):
            lines = pl.ds(x * ROWS, ROWS)
            value = section[c, lines] + placed[x * ROWS : (x + 1) * ROWS] + axial_in[0, x, c] + axial_in[1, x, c]
            section[c, lines] = value
            modulated[pl.ds(c * LINES + x * ROWS, ROWS), 0:WIDTH] = value * wave_c
            modulated[pl.ds(c * LINES + x * ROWS, ROWS), WIDTH : 2 * WIDTH] = value * wave_s
    messages = matmul(sources, modulated[...], ((1,), (1,)))
    message_out[...] = messages[0:MESSAGE_ROWS]
    spans = (
        (pl.ds(2 * NEAR_ROWS, FAR_ROWS), across),
        (pl.ds(0, NEAR_ROWS), right),
        (pl.ds(NEAR_ROWS, NEAR_ROWS), left),
    )
    message_copies = []
    for slot, (span, sector) in enumerate(spans, 7):
        copy = remote(message_out.at[span], message_in.at[span], slot, (ax, sector))
        copy.start()
        message_copies.append(copy)

    basis = tab("basis")
    for c in range(FIELDS):
        coefficients = matmul(section[c], basis)
        weighted = coefficients * jnp.concatenate([ring_weight] * STATIONS, axis=0)
        smoothed = matmul(weighted, basis, ((1,), (1,)))
        for x in range(STATIONS):
            modulated[pl.ds(c * LINES + x * ROWS, ROWS), 0:WIDTH] = smoothed[x * ROWS : (x + 1) * ROWS]

    part_row = lax.broadcasted_iota(jnp.int32, (64, 2 * WIDTH), 0)
    sign_left = jnp.where(az == 0, -1.0, 1.0)
    sign_right = jnp.where(az == SECTORS - 1, -1.0, 1.0)
    sign_across = jnp.where(az < 2, -1.0, 1.0)
    signs = jnp.where(part_row < NEAR_ROWS, sign_left, jnp.where(part_row < 2 * NEAR_ROWS, sign_right, sign_across))
    targets = jnp.concatenate([tab("target_a"), tab("target_b")], axis=1) * signs.astype(jnp.float32)

    extra_left.wait_recv()
    extra_right.wait_recv()
    extra = jnp.concatenate([extra_in[...], extra_own[...]], axis=0)
    extra_field = matmul(extra, targets, ((0,), (0,)))
    mirror_copy.wait_recv()
    mirrored = mirror_in[...]
    weighted = matmul(mirrored, basis) * jnp.concatenate([inner_weight] * 10, axis=0)
    compact_smooth = matmul(weighted, basis, ((1,), (1,)))
    for c in range(FIELDS):
        for half in range(2):
            lines = pl.ds(16 * c + 8 * half, 8)
            low = 16 * c + 8 * half
            smooth = (
                compact_smooth[low : low + 8]
                + inner_s * extra_field[low : low + 8, 0:WIDTH]
                + inner_c * extra_field[low : low + 8, WIDTH : 2 * WIDTH]
            )
            limit = jnp.where(row < 4, counts[2 * half], counts[2 * half + 1])
            compact[lines] = jnp.where((row & 3) < limit, smooth, mirror_in[lines])

    for copy in message_copies:
        copy.wait_recv()
    for c in range(FIELDS):
        field = matmul(message_in[:, c * LINES : (c + 1) * LINES], targets[0:MESSAGE_ROWS], ((0,), (0,)))
        for x in range(STATIONS):
            low = x * ROWS
            smooth = (
                modulated[pl.ds(c * LINES + low, ROWS), 0:WIDTH]
                + wave_s * field[low : low + ROWS, 0:WIDTH]
                + wave_c * field[low : low + ROWS, WIDTH : 2 * WIDTH]
            )
            out[x, c] = jnp.where(ring_row < counts[x], smooth, section[c, pl.ds(low, ROWS)])
            out[x, c, 0:4] += compact[pl.ds(16 * c + 4 * x, 4)]

    pl.when(has_high)(to_high.wait_send)
    pl.when(has_low)(to_low.wait_send)
    for copy in (edge_left, edge_right, mirror_copy, extra_left, extra_right, *message_copies):
        copy.wait_send()


def store(ref, index, value):
    ref[index] = value


def to_low_wait(copy):
    return copy.wait_recv


def per_device(conserved, cycle_modes, filtered_cycles):
    f32 = jnp.float32
    block = (STATIONS, FIELDS, ROWS, WIDTH)
    lines = FIELDS * LINES
    return pl.pallas_call(
        body,
        out_shape=jax.ShapeDtypeStruct(block, f32),
        in_specs=[
            pl.BlockSpec(memory_space=pl.ANY),
            pl.BlockSpec(memory_space=pl.ANY),
            pl.BlockSpec(memory_space=pltpu.SMEM),
            pl.BlockSpec(memory_space=pltpu.SMEM),
        ],
        out_specs=pl.BlockSpec(memory_space=pltpu.VMEM),
        scratch_shapes=[
            pltpu.VMEM(block, f32),
            pltpu.VMEM(TABLES.shape, f32),
            pltpu.VMEM(block, f32),
            pltpu.VMEM((FIELDS, LINES, WIDTH), f32),
            pltpu.VMEM((FIELDS, LINES, WIDTH), f32),
            pltpu.VMEM((2,) + block, f32),
            pltpu.VMEM((2,) + block, f32),
            pltpu.VMEM((2, 4, lines), f32),
            pltpu.VMEM((2, 4, lines), f32),
            pltpu.VMEM((80, WIDTH), f32),
            pltpu.VMEM((80, WIDTH), f32),
            pltpu.VMEM((128, 2 * WIDTH), f32),
            pltpu.VMEM((2 * NEAR_ROWS, WIDTH), f32),
            pltpu.VMEM((2 * NEAR_ROWS, WIDTH), f32),
            pltpu.VMEM((16, WIDTH), f32),
            pltpu.VMEM((FIELDS, LINES, WIDTH), f32),
            pltpu.VMEM((lines, 2 * WIDTH), f32),
            pltpu.VMEM((MESSAGE_ROWS, lines), f32),
            pltpu.VMEM((MESSAGE_ROWS, lines), f32),
            pltpu.VMEM((80, WIDTH), f32),
            pltpu.SemaphoreType.DMA((2,)),
            pltpu.SemaphoreType.DMA((10,)),
            pltpu.SemaphoreType.DMA((10,)),
        ],
        compiler_params=pltpu.CompilerParams(
            collective_id=0, has_side_effects=True, vmem_limit_bytes=32 * 1024 * 1024
        ),
    )(conserved, jnp.asarray(TABLES), cycle_modes, filtered_cycles)


def solution(mesh):
    placed = (P("ax", None, None, "az"), P(), P("ax"))
    return jax.shard_map(
        per_device, mesh=mesh, in_specs=placed, out_specs=P("ax", None, None, "az"), check_vma=False
    )
```

time: 244 us -> 69.4 us (0.28)
  the two profiles are of different devices: /device:TPU:39 before, /device:TPU:32 now
where the time goes in v1:
time: 69.4 us; the launch traced here: 69.1 us
  Pallas kernels  65.1 us (94%)
  local copies, waits for them, and re-layouts  3.99 us (6%)
    pallas_call x1, Pallas kernels, per_device(): pl.pallas_call(body, out_shape=jax.ShapeDtypeStruct(block, f32), in_specs...  65.1 us
    unnamed x9, local copies, waits for them, and re-layouts  3.99 us

profile of v1, /device:TPU:32, one launch (start us, length us, event | category | flops | bytes accessed | tf_op | source)
XLA Modules:
  0.0 69.1 jit_solution(16072454651299198978)
XLA Ops:
  0.0 0.0 copy-start
  0.0 1.0 %copy-done = f32[672,128]{1,0:T(8,128)S(1)} copy-done((f32[672,128]{1,0:T(8,128)S(1)}, f32[672,128]{1,0:T(8,128)}, u32[]{:S(2)}) %copy-start) | copy-done | bytes 344088
  1.0 0.0 copy-start.1
  1.0 1.0 %copy-done.1 = f32[4,5,32,128]{3,2,1,0:T(8,128)S(1)} copy-done((f32[4,5,32,128]{3,2,1,0:T(8,128)S(1)}, f32[4,5,32,128]{3,2,1,0:T(8,128)}, u32[]{:S(2)}) %copy-start.1) | copy-done | bytes 327704
  2.0 0.0 copy-start.2
  2.0 0.7 copy-done.2
  2.6 0.0 copy-start.3
  2.6 0.7 copy-done.3
  3.3 65.1 %shard_map.46 = f32[4,5,32,128]{3,2,1,0:T(8,128)S(1)} custom-call(f32[4,5,32,128]{3,2,1,0:T(8,128)S(1)} %copy-done.1, f32[672,128]{1,0:T(8,128)S(1)} %copy-done, s32[32]{0:T(128)S(1)} %copy-done.2, s32[4]{0:T(128)S(1)} %copy-done.3), custom_call_target="tpu_custom_call" | custom-call | tf_op jit(solution)/shard_map/pallas_call | solution.py:365
  68.4 0.7 %copy.6 = f32[4,5,32,128]{3,2,1,0:T(8,128)} copy(f32[4,5,32,128]{3,2,1,0:T(8,128)S(1)} %shard_map.46) | data formatting | bytes 655360
Async XLA Ops:
  0.0 1.0 %copy-start = (f32[672,128]{1,0:T(8,128)S(1)}, f32[672,128]{1,0:T(8,128)}, u32[]{:S(2)}) copy-start(f32[672,128]{1,0:T(8,128)} %constant.2.clone.tables) | copy-start | bytes 1032196
  1.0 1.0 %copy-start.1 = (f32[4,5,32,128]{3,2,1,0:T(8,128)S(1)}, f32[4,5,32,128]{3,2,1,0:T(8,128)}, u32[]{:S(2)}) copy-start(f32[4,5,32,128]{3,2,1,0:T(8,128)} %conserved.1) | copy-start | bytes 983044
  2.0 0.7 copy-start.2
  2.6 0.7 copy-start.3

commit v2 on v1

--- a/solution.py
+++ b/solution.py
@@ -22,8 +22,8 @@
 FIELDS = 5
 ROWS = 32
 LINES = STATIONS * ROWS
-NEAR = 12
-FAR = 6
+NEAR = 11
+FAR = 5
 MESH = pl.DeviceIdType.MESH
 EXACT = lax.Precision.HIGHEST
 MIRROR_SIGNS = (1.0, 1.0, -1.0, -1.0, 1.0)
@@ -35,6 +35,12 @@
     left, values, right = np.linalg.svd(1.0 / np.sin(np.pi * gap / NT))
     root = np.sqrt(values[:rank])
     return (left[:, :rank] * root).T, right[:rank] * root[:, None]
+
+
+NEAR_ROWS = 2 * NEAR
+FAR_ROWS = 2 * FAR
+NEAR_PAD = 24
+MESSAGE_ROWS = 64
 
 
 def build_tables():
@@ -77,14 +83,12 @@
     source_b = np.zeros((64, WIDTH))
     target_a = np.zeros((64, WIDTH))
     target_b = np.zeros((64, WIDTH))
-    first = 0
-    for distance, rank in ((1, NEAR), (-1, NEAR), (2, FAR)):
+    for distance, rank, first in ((1, NEAR, 0), (-1, NEAR, NEAR_PAD), (2, FAR, 2 * NEAR_PAD)):
         target, source = kernel_factors(distance, rank)
         source_a[first : first + rank] = source
         source_b[first + rank : first + 2 * rank] = source
         target_a[first : first + rank] = target / NT
         target_b[first + rank : first + 2 * rank] = -target / NT
-        first += 2 * rank
     parts["source_a"] = source_a
     parts["source_b"] = source_b
     parts["target_a"] = target_a
@@ -98,9 +102,6 @@
 
 
 TABLES, SPANS = build_tables()
-NEAR_ROWS = 2 * NEAR
-FAR_ROWS = 2 * FAR
-MESSAGE_ROWS = 2 * NEAR_ROWS + FAR_ROWS
 
 
 def matmul(left, right, dims=((1,), (0,))):
@@ -116,9 +117,9 @@
 
 def body(
     conserved, tables, modes, counts, out,
-    cells, table, flux_f, flux_g, flux_h,
+    cells, table, mode, count, flux_f, flux_g, flux_h,
     axial_out, axial_in, edge_out, edge_in, mirror_out, mirror_in, mirror_mod,
-    extra_out, extra_in, extra_own, section, modulated, message_out, message_in, compact,
+    extra_out, extra_in, extra_own, section, modulated, near_out, near_in, far_out, far_in, message, compact,
     load_sem, send_sem, recv_sem,
 ):
     ax = lax.axis_index("ax")
@@ -131,7 +132,7 @@
     has_high = ax < ax_count - 1
 
     barrier = pltpu.get_barrier_semaphore()
-    for sector in (right, left, across):
+    for sector in (right, left):
         pl.semaphore_signal(barrier, inc=1, device_id=(ax, sector), device_id_type=MESH)
 
     @pl.when(has_low)
@@ -144,6 +145,10 @@
 
     load_cells = pltpu.make_async_copy(conserved, cells, load_sem.at[0])
     load_table = pltpu.make_async_copy(tables, table, load_sem.at[1])
+    load_mode = pltpu.make_async_copy(modes, mode, load_sem.at[2])
+    load_count = pltpu.make_async_copy(counts, count, load_sem.at[3])
+    load_mode.start()
+    load_count.start()
     load_cells.start()
     load_table.start()
 
@@ -153,16 +158,21 @@
 
     row = lax.broadcasted_iota(jnp.int32, (8, WIDTH), 0)
     lane = lax.broadcasted_iota(jnp.int32, (8, WIDTH), 1)
+    lines_all = FIELDS * LINES
+    for low, high in ((NEAR_ROWS, NEAR_PAD), (NEAR_PAD + NEAR_ROWS, 2 * NEAR_PAD), (2 * NEAR_PAD + FAR_ROWS, MESSAGE_ROWS)):
+        message[low:high] = jnp.zeros((high - low, lines_all), jnp.float32)
+    load_mode.wait()
+    load_count.wait()
     mode_tiles = []
     for tile in range(ROWS // 8):
         value = jnp.zeros((8, WIDTH), jnp.int32)
         for j in range(8):
-            value = jnp.where(row == j, modes[tile * 8 + j], value)
+            value = jnp.where(row == j, mode[tile * 8 + j], value)
         mode_tiles.append(value)
     ring_modes = jnp.concatenate(mode_tiles, axis=0)
     inner_modes = jnp.zeros((8, WIDTH), jnp.int32)
     for j in range(4):
-        inner_modes = jnp.where((row & 3) == j, modes[j], inner_modes)
+        inner_modes = jnp.where((row & 3) == j, mode[j], inner_modes)
     wave_c, wave_s = sector_waves(ring_modes, az)
     inner_c, inner_s = sector_waves(inner_modes, az)
     across_c, across_s = sector_waves(inner_modes, across)
@@ -231,15 +241,15 @@
             device_id=device, device_id_type=MESH,
         )
 
-    pl.semaphore_wait(barrier, 3 + has_low.astype(jnp.int32) + has_high.astype(jnp.int32))
+    pl.semaphore_wait(barrier, 2 + has_low.astype(jnp.int32) + has_high.astype(jnp.int32))
     to_high = remote(axial_out.at[1], axial_in.at[0], 0, (ax + 1, az))
     to_low = remote(axial_out.at[0], axial_in.at[1], 1, (ax - 1, az))
-    pl.when(has_high)(to_high.start)
-    pl.when(has_low)(to_low.start)
     edge_left = remote(edge_out.at[0], edge_in.at[0], 2, (ax, left))
     edge_right = remote(edge_out.at[1], edge_in.at[1], 3, (ax, right))
     edge_left.start()
     edge_right.start()
+    pl.when(has_high)(to_high.start)
+    pl.when(has_low)(to_low.start)
 
     mirror_table = tab("mirror")
     for c in range(FIELDS):
@@ -251,14 +261,13 @@
             mirror_mod[lines, WIDTH : 2 * WIDTH] = value[8 * half : 8 * half + 8] * across_s
     mirror_mod[80:128] = jnp.zeros((48, 2 * WIDTH), jnp.float32)
     mirror_copy = remote(mirror_out, mirror_in, 4, (ax, across))
-    mirror_copy.start()
     sources = jnp.concatenate([tab("source_a"), tab("source_b")], axis=1)
     extra = matmul(sources, mirror_mod[...], ((1,), (1,)))
-    extra_out[...] = extra[0 : 2 * NEAR_ROWS]
-    extra_own[...] = extra[2 * NEAR_ROWS : 64]
-    extra_left = remote(extra_out.at[0:NEAR_ROWS], extra_in.at[0:NEAR_ROWS], 5, (ax, left))
+    extra_out[...] = extra[0 : 2 * NEAR_PAD]
+    extra_own[...] = extra[2 * NEAR_PAD : 64]
+    extra_left = remote(extra_out.at[0:NEAR_PAD], extra_in.at[0:NEAR_PAD], 5, (ax, left))
     extra_right = remote(
-        extra_out.at[NEAR_ROWS : 2 * NEAR_ROWS], extra_in.at[NEAR_ROWS : 2 * NEAR_ROWS], 6, (ax, right)
+        extra_out.at[NEAR_PAD : 2 * NEAR_PAD], extra_in.at[NEAR_PAD : 2 * NEAR_PAD], 6, (ax, right)
     )
     extra_left.start()
     extra_right.start()
@@ -270,6 +279,9 @@
 
     pl.when(has_high)(to_low_wait(remote(axial_out.at[1], axial_in.at[1], 1, (ax + 1, az))))
     pl.when(has_low)(to_low_wait(remote(axial_out.at[0], axial_in.at[0], 0, (ax - 1, az))))
+    for c in range(FIELDS):
+        for x in range(STATIONS):
+            section[c, pl.ds(x * ROWS, ROWS)] += axial_in[0, x, c] + axial_in[1, x, c]
     edge_left.wait_recv()
     edge_right.wait_recv()
     edges = jnp.concatenate([edge_in[0], edge_in[1]], axis=0)
@@ -278,22 +290,21 @@
         placed = matmul(edges[:, c * LINES : (c + 1) * LINES], place, ((0,), (0,)))
         for x in range(STATIONS):
             lines = pl.ds(x * ROWS, ROWS)
-            value = section[c, lines] + placed[x * ROWS : (x + 1) * ROWS] + axial_in[0, x, c] + axial_in[1, x, c]
+            value = section[c, lines] + placed[x * ROWS : (x + 1) * ROWS]
             section[c, lines] = value
             modulated[pl.ds(c * LINES + x * ROWS, ROWS), 0:WIDTH] = value * wave_c
             modulated[pl.ds(c * LINES + x * ROWS, ROWS), WIDTH : 2 * WIDTH] = value * wave_s
     messages = matmul(sources, modulated[...], ((1,), (1,)))
-    message_out[...] = messages[0:MESSAGE_ROWS]
-    spans = (
-        (pl.ds(2 * NEAR_ROWS, FAR_ROWS), across),
-        (pl.ds(0, NEAR_ROWS), right),
-        (pl.ds(NEAR_ROWS, NEAR_ROWS), left),
-    )
-    message_copies = []
-    for slot, (span, sector) in enumerate(spans, 7):
-        copy = remote(message_out.at[span], message_in.at[span], slot, (ax, sector))
-        copy.start()
-        message_copies.append(copy)
+    far_out[...] = messages[2 * NEAR_PAD : 2 * NEAR_PAD + FAR_ROWS]
+    far_copy = remote(far_out, far_in, 7, (ax, across))
+    far_copy.start()
+    mirror_copy.start()
+    near_out[0] = messages[0:NEAR_ROWS]
+    near_right = remote(near_out.at[0], near_in.at[0], 8, (ax, right))
+    near_right.start()
+    near_out[1] = messages[NEAR_PAD : NEAR_PAD + NEAR_ROWS]
+    near_left = remote(near_out.at[1], near_in.at[1], 9, (ax, left))
+    near_left.start()
 
     basis = tab("basis")
     for c in range(FIELDS):
@@ -307,7 +318,7 @@
     sign_left = jnp.where(az == 0, -1.0, 1.0)
     sign_right = jnp.where(az == SECTORS - 1, -1.0, 1.0)
     sign_across = jnp.where(az < 2, -1.0, 1.0)
-    signs = jnp.where(part_row < NEAR_ROWS, sign_left, jnp.where(part_row < 2 * NEAR_ROWS, sign_right, sign_across))
+    signs = jnp.where(part_row < NEAR_PAD, sign_left, jnp.where(part_row < 2 * NEAR_PAD, sign_right, sign_across))
     targets = jnp.concatenate([tab("target_a"), tab("target_b")], axis=1) * signs.astype(jnp.float32)
 
     extra_left.wait_recv()
@@ -327,13 +338,17 @@
                 + inner_s * extra_field[low : low + 8, 0:WIDTH]
                 + inner_c * extra_field[low : low + 8, WIDTH : 2 * WIDTH]
             )
-            limit = jnp.where(row < 4, counts[2 * half], counts[2 * half + 1])
+            limit = jnp.where(row < 4, count[2 * half], count[2 * half + 1])
             compact[lines] = jnp.where((row & 3) < limit, smooth, mirror_in[lines])
 
-    for copy in message_copies:
-        copy.wait_recv()
-    for c in range(FIELDS):
-        field = matmul(message_in[:, c * LINES : (c + 1) * LINES], targets[0:MESSAGE_ROWS], ((0,), (0,)))
+    far_copy.wait_recv()
+    message[2 * NEAR_PAD : 2 * NEAR_PAD + FAR_ROWS] = far_in[...]
+    near_right.wait_recv()
+    message[0:NEAR_ROWS] = near_in[0]
+    near_left.wait_recv()
+    message[NEAR_PAD : NEAR_PAD + NEAR_ROWS] = near_in[1]
+    for c in range(FIELDS):
+        field = matmul(message[:, c * LINES : (c + 1) * LINES], targets, ((0,), (0,)))
         for x in range(STATIONS):
             low = x * ROWS
             smooth = (
@@ -341,12 +356,12 @@
                 + wave_s * field[low : low + ROWS, 0:WIDTH]
                 + wave_c * field[low : low + ROWS, WIDTH : 2 * WIDTH]
             )
-            out[x, c] = jnp.where(ring_row < counts[x], smooth, section[c, pl.ds(low, ROWS)])
+            out[x, c] = jnp.where(ring_row < count[x], smooth, section[c, pl.ds(low, ROWS)])
             out[x, c, 0:4] += compact[pl.ds(16 * c + 4 * x, 4)]
 
     pl.when(has_high)(to_high.wait_send)
     pl.when(has_low)(to_low.wait_send)
-    for copy in (edge_left, edge_right, mirror_copy, extra_left, extra_right, *message_copies):
+    for copy in (edge_left, edge_right, mirror_copy, extra_left, extra_right, far_copy, near_right, near_left):
         copy.wait_send()
 
 
@@ -366,15 +381,17 @@
         body,
         out_shape=jax.ShapeDtypeStruct(block, f32),
         in_specs=[
-            pl.BlockSpec(memory_space=pl.ANY),
-            pl.BlockSpec(memory_space=pl.ANY),
-            pl.BlockSpec(memory_space=pltpu.SMEM),
-            pl.BlockSpec(memory_space=pltpu.SMEM),
+            pl.BlockSpec(memory_space=pltpu.HBM),
+            pl.BlockSpec(memory_space=pltpu.HBM),
+            pl.BlockSpec(memory_space=pltpu.HBM),
+            pl.BlockSpec(memory_space=pltpu.HBM),
         ],
         out_specs=pl.BlockSpec(memory_space=pltpu.VMEM),
         scratch_shapes=[
             pltpu.VMEM(block, f32),
             pltpu.VMEM(TABLES.shape, f32),
+            pltpu.SMEM((ROWS,), jnp.int32),
+            pltpu.SMEM((STATIONS,), jnp.int32),
             pltpu.VMEM(block, f32),
             pltpu.VMEM((FIELDS, LINES, WIDTH), f32),
             pltpu.VMEM((FIELDS, LINES, WIDTH), f32),
@@ -385,20 +402,23 @@
             pltpu.VMEM((80, WIDTH), f32),
             pltpu.VMEM((80, WIDTH), f32),
             pltpu.VMEM((128, 2 * WIDTH), f32),
-            pltpu.VMEM((2 * NEAR_ROWS, WIDTH), f32),
-            pltpu.VMEM((2 * NEAR_ROWS, WIDTH), f32),
+            pltpu.VMEM((2 * NEAR_PAD, WIDTH), f32),
+            pltpu.VMEM((2 * NEAR_PAD, WIDTH), f32),
             pltpu.VMEM((16, WIDTH), f32),
             pltpu.VMEM((FIELDS, LINES, WIDTH), f32),
             pltpu.VMEM((lines, 2 * WIDTH), f32),
-            pltpu.VMEM((MESSAGE_ROWS, lines), f32),
+            pltpu.VMEM((2, NEAR_ROWS, lines), f32),
+            pltpu.VMEM((2, NEAR_ROWS, lines), f32),
+            pltpu.VMEM((FAR_ROWS, lines), f32),
+            pltpu.VMEM((FAR_ROWS, lines), f32),
             pltpu.VMEM((MESSAGE_ROWS, lines), f32),
             pltpu.VMEM((80, WIDTH), f32),
-            pltpu.SemaphoreType.DMA((2,)),
+            pltpu.SemaphoreType.DMA((4,)),
             pltpu.SemaphoreType.DMA((10,)),
             pltpu.SemaphoreType.DMA((10,)),
         ],
         compiler_params=pltpu.CompilerParams(
-            collective_id=0, has_side_effects=True, vmem_limit_bytes=32 * 1024 * 1024
+            collective_id=0, has_side_effects=True, vmem_limit_bytes=60 * 1024 * 1024
         ),
     )(conserved, jnp.asarray(TABLES), cycle_modes, filtered_cycles)
 

time: 69.4 us -> 67.5 us (0.973)
  the two profiles are of different devices: /device:TPU:32 before, /device:TPU:46 now
where the time goes in v2:
time: 67.5 us; the launch traced here: 67.3 us
  Pallas kernels  65.5 us (97%)
  local copies, waits for them, and re-layouts  1.72 us (3%)
    pallas_call x1, Pallas kernels, per_device(): pl.pallas_call(body, out_shape=jax.ShapeDtypeStruct(block, f32), in_specs...  65.5 us
    unnamed x1, local copies, waits for them, and re-layouts  1.72 us

profile of v2, /device:TPU:46, one launch (start us, length us, event | category | flops | bytes accessed | tf_op | source)
XLA Modules:
  0.0 67.3 jit_solution(13307636256302267659)
XLA Ops:
  0.0 65.5 %shard_map.46 = f32[4,5,32,128]{3,2,1,0:T(8,128)} custom-call(f32[4,5,32,128]{3,2,1,0:T(8,128)} %conserved.1, f32[672,128]{1,0:T(8,128)} %constant.2.clone.tables, s32[32]{0:T(128)} %modes.1, s32[4]{0:T(128)} %counts.1), custom_call_target="tpu_custom_call" | custom-call | tf_op jit(solution)/shard_map/pallas_call | solution.py:380
  65.5 1.7 %copy.6 = f32[4,5,32,128]{3,2,1,0:T(8,128)} copy(f32[4,5,32,128]{3,2,1,0:T(8,128)} %shard_map.46) | data formatting | bytes 655360

commit v3 on v2

--- a/solution.py
+++ b/solution.py
@@ -22,16 +22,15 @@
 FIELDS = 5
 ROWS = 32
 LINES = STATIONS * ROWS
-NEAR = 11
+NEAR = 10
 FAR = 5
 MESH = pl.DeviceIdType.MESH
 EXACT = lax.Precision.HIGHEST
 MIRROR_SIGNS = (1.0, 1.0, -1.0, -1.0, 1.0)
 
 
-def kernel_factors(distance, rank):
-    cells = np.arange(WIDTH)
-    gap = WIDTH * distance + cells[:, None] - cells[None, :]
+def kernel_factors(distance, rank, sources):
+    gap = WIDTH * distance + np.arange(WIDTH)[:, None] - sources[None, :]
     left, values, right = np.linalg.svd(1.0 / np.sin(np.pi * gap / NT))
     root = np.sqrt(values[:rank])
     return (left[:, :rank] * root).T, right[:rank] * root[:, None]
@@ -83,14 +82,30 @@
     source_b = np.zeros((64, WIDTH))
     target_a = np.zeros((64, WIDTH))
     target_b = np.zeros((64, WIDTH))
-    for distance, rank, first in ((1, NEAR, 0), (-1, NEAR, NEAR_PAD), (2, FAR, 2 * NEAR_PAD)):
-        target, source = kernel_factors(distance, rank)
-        source_a[first : first + rank] = source
-        source_b[first + rank : first + 2 * rank] = source
-        target_a[first : first + rank] = target / NT
-        target_b[first + rank : first + 2 * rank] = -target / NT
+    source_edge = np.zeros((2 * MESSAGE_ROWS, WIDTH))
+    for distance, rank, first, low, high in (
+        (1, NEAR, 0, -4, WIDTH),
+        (-1, NEAR, NEAR_PAD, 0, WIDTH + 4),
+        (2, FAR, 2 * NEAR_PAD, -4, WIDTH + 4),
+    ):
+        target, source = kernel_factors(distance, rank, np.arange(low, high))
+        own = source[:, -low : WIDTH - low]
+        for wave, (into, out_of, half) in enumerate(((source_a, target_a, 1.0 / NT), (source_b, target_b, -1.0 / NT))):
+            rows = slice(first + wave * rank, first + (wave + 1) * rank)
+            back = slice(MESSAGE_ROWS + rows.start, MESSAGE_ROWS + rows.stop)
+            into[rows] = own
+            out_of[rows] = half * target
+            if low < 0:
+                source_edge[rows, 8 * wave : 8 * wave + 4] = source[:, 0:4]
+            if high > WIDTH:
+                source_edge[rows, 8 * wave + 4 : 8 * wave + 8] = source[:, -4:]
+            if distance == 1:
+                source_edge[back, 8 * wave : 8 * wave + 4] = own[:, -4:]
+            if distance == -1:
+                source_edge[back, 8 * wave + 4 : 8 * wave + 8] = own[:, 0:4]
     parts["source_a"] = source_a
     parts["source_b"] = source_b
+    parts["source_edge"] = source_edge
     parts["target_a"] = target_a
     parts["target_b"] = target_b
     spans, blocks, start = {}, [], 0
@@ -109,7 +124,10 @@
 
 
 def sector_waves(modes, sector):
-    cell = lax.broadcasted_iota(jnp.int32, modes.shape, 1) + sector * WIDTH
+    return waves(modes, lax.broadcasted_iota(jnp.int32, modes.shape, 1) + sector * WIDTH)
+
+
+def waves(modes, cell):
     turn = ((2 * modes - 1) * cell) & (2 * NT - 1)
     angle = turn.astype(jnp.float32) * (math.pi / NT)
     return jnp.cos(angle), jnp.sin(angle)
@@ -119,8 +137,8 @@
     conserved, tables, modes, counts, out,
     cells, table, mode, count, flux_f, flux_g, flux_h,
     axial_out, axial_in, edge_out, edge_in, mirror_out, mirror_in, mirror_mod,
-    extra_out, extra_in, extra_own, section, modulated, near_out, near_in, far_out, far_in, message, compact,
-    load_sem, send_sem, recv_sem,
+    extra_out, extra_in, extra_own, section, modulated, near_out, near_in, far_out, far_in, message, from_edges, compact,
+    load_sem, send_sem, recv_sem, go_sem,
 ):
     ax = lax.axis_index("ax")
     az = lax.axis_index("az")
@@ -173,6 +191,10 @@
     inner_modes = jnp.zeros((8, WIDTH), jnp.int32)
     for j in range(4):
         inner_modes = jnp.where((row & 3) == j, mode[j], inner_modes)
+    line_modes = jnp.zeros((8, WIDTH), jnp.int32)
+    for j in range(ROWS):
+        line_modes = jnp.where((lane & (ROWS - 1)) == j, mode[j], line_modes)
+    edge_c, edge_s = waves(line_modes, az * WIDTH + row + jnp.where(row < 4, -4, WIDTH - 4))
     wave_c, wave_s = sector_waves(ring_modes, az)
     inner_c, inner_s = sector_waves(inner_modes, az)
     across_c, across_s = sector_waves(inner_modes, across)
@@ -234,23 +256,10 @@
     edges = matmul(tab("edge"), flux_h[...].reshape(FIELDS * LINES, WIDTH), ((1,), (1,)))
     edge_out[0] = edges[0:4]
     edge_out[1] = edges[4:8]
-
-    def remote(source, target, slot, device):
-        return pltpu.make_async_remote_copy(
-            src_ref=source, dst_ref=target, send_sem=send_sem.at[slot], recv_sem=recv_sem.at[slot],
-            device_id=device, device_id_type=MESH,
-        )
-
-    pl.semaphore_wait(barrier, 2 + has_low.astype(jnp.int32) + has_high.astype(jnp.int32))
-    to_high = remote(axial_out.at[1], axial_in.at[0], 0, (ax + 1, az))
-    to_low = remote(axial_out.at[0], axial_in.at[1], 1, (ax - 1, az))
-    edge_left = remote(edge_out.at[0], edge_in.at[0], 2, (ax, left))
-    edge_right = remote(edge_out.at[1], edge_in.at[1], 3, (ax, right))
-    edge_left.start()
-    edge_right.start()
-    pl.when(has_high)(to_high.start)
-    pl.when(has_low)(to_low.start)
-
+    edge_waves = jnp.concatenate(
+        [edges * jnp.concatenate([edge_c] * FIELDS, axis=1), edges * jnp.concatenate([edge_s] * FIELDS, axis=1)], axis=0
+    )
+    from_edges[...] = matmul(tab("source_edge")[:, 0:16], edge_waves)
     mirror_table = tab("mirror")
     for c in range(FIELDS):
         value = MIRROR_SIGNS[c] * matmul(mirror_table, flux_g[c])
@@ -260,51 +269,69 @@
             mirror_mod[lines, 0:WIDTH] = value[8 * half : 8 * half + 8] * across_c
             mirror_mod[lines, WIDTH : 2 * WIDTH] = value[8 * half : 8 * half + 8] * across_s
     mirror_mod[80:128] = jnp.zeros((48, 2 * WIDTH), jnp.float32)
-    mirror_copy = remote(mirror_out, mirror_in, 4, (ax, across))
     sources = jnp.concatenate([tab("source_a"), tab("source_b")], axis=1)
     extra = matmul(sources, mirror_mod[...], ((1,), (1,)))
     extra_out[...] = extra[0 : 2 * NEAR_PAD]
     extra_own[...] = extra[2 * NEAR_PAD : 64]
+    radial_table = tab("radial")
+    swirl_table = tab("swirl")
+    for c in range(FIELDS):
+        section[c] += matmul(radial_table, flux_g[c]) + matmul(flux_h[c], swirl_table)
+
+    def remote(source, target, slot, device):
+        return pltpu.make_async_remote_copy(
+            src_ref=source, dst_ref=target, send_sem=send_sem.at[slot], recv_sem=recv_sem.at[slot],
+            device_id=device, device_id_type=MESH,
+        )
+
+    pl.semaphore_wait(barrier, 2 + has_low.astype(jnp.int32) + has_high.astype(jnp.int32))
+    to_high = remote(axial_out.at[1], axial_in.at[0], 0, (ax + 1, az))
+    to_low = remote(axial_out.at[0], axial_in.at[1], 1, (ax - 1, az))
+    edge_left = remote(edge_out.at[0], edge_in.at[0], 2, (ax, left))
+    edge_right = remote(edge_out.at[1], edge_in.at[1], 3, (ax, right))
     extra_left = remote(extra_out.at[0:NEAR_PAD], extra_in.at[0:NEAR_PAD], 5, (ax, left))
     extra_right = remote(
         extra_out.at[NEAR_PAD : 2 * NEAR_PAD], extra_in.at[NEAR_PAD : 2 * NEAR_PAD], 6, (ax, right)
     )
+    mirror_copy = remote(mirror_out, mirror_in, 4, (ax, across))
+    far_copy = remote(far_out, far_in, 7, (ax, across))
+    near_right = remote(near_out.at[0], near_in.at[0], 8, (ax, right))
+    near_left = remote(near_out.at[1], near_in.at[1], 9, (ax, left))
+    for sector in (right, left):
+        pl.semaphore_signal(go_sem, inc=1, device_id=(ax, sector), device_id_type=MESH)
+    edge_left.start()
+    edge_right.start()
+    pl.when(has_high)(to_high.start)
+    pl.when(has_low)(to_low.start)
     extra_left.start()
     extra_right.start()
-
-    radial_table = tab("radial")
-    swirl_table = tab("swirl")
-    for c in range(FIELDS):
-        section[c] += matmul(radial_table, flux_g[c]) + matmul(flux_h[c], swirl_table)
+    pl.semaphore_wait(go_sem, 2)
+    mirror_copy.start()
 
     pl.when(has_high)(to_low_wait(remote(axial_out.at[1], axial_in.at[1], 1, (ax + 1, az))))
     pl.when(has_low)(to_low_wait(remote(axial_out.at[0], axial_in.at[0], 0, (ax - 1, az))))
     for c in range(FIELDS):
         for x in range(STATIONS):
-            section[c, pl.ds(x * ROWS, ROWS)] += axial_in[0, x, c] + axial_in[1, x, c]
+            lines = pl.ds(x * ROWS, ROWS)
+            value = section[c, lines] + axial_in[0, x, c] + axial_in[1, x, c]
+            section[c, lines] = value
+            modulated[pl.ds(c * LINES + x * ROWS, ROWS), 0:WIDTH] = value * wave_c
+            modulated[pl.ds(c * LINES + x * ROWS, ROWS), WIDTH : 2 * WIDTH] = value * wave_s
+    messages = matmul(sources, modulated[...], ((1,), (1,))) + from_edges[0:MESSAGE_ROWS]
+    far_out[...] = messages[2 * NEAR_PAD : 2 * NEAR_PAD + FAR_ROWS]
+    near_out[0] = messages[0:NEAR_ROWS]
+    near_out[1] = messages[NEAR_PAD : NEAR_PAD + NEAR_ROWS]
+    far_copy.start()
+    mirror_copy.wait_send()
+    near_right.start()
+    near_left.start()
+
     edge_left.wait_recv()
     edge_right.wait_recv()
     edges = jnp.concatenate([edge_in[0], edge_in[1]], axis=0)
     place = tab("place")
     for c in range(FIELDS):
-        placed = matmul(edges[:, c * LINES : (c + 1) * LINES], place, ((0,), (0,)))
-        for x in range(STATIONS):
-            lines = pl.ds(x * ROWS, ROWS)
-            value = section[c, lines] + placed[x * ROWS : (x + 1) * ROWS]
-            section[c, lines] = value
-            modulated[pl.ds(c * LINES + x * ROWS, ROWS), 0:WIDTH] = value * wave_c
-            modulated[pl.ds(c * LINES + x * ROWS, ROWS), WIDTH : 2 * WIDTH] = value * wave_s
-    messages = matmul(sources, modulated[...], ((1,), (1,)))
-    far_out[...] = messages[2 * NEAR_PAD : 2 * NEAR_PAD + FAR_ROWS]
-    far_copy = remote(far_out, far_in, 7, (ax, across))
-    far_copy.start()
-    mirror_copy.start()
-    near_out[0] = messages[0:NEAR_ROWS]
-    near_right = remote(near_out.at[0], near_in.at[0], 8, (ax, right))
-    near_right.start()
-    near_out[1] = messages[NEAR_PAD : NEAR_PAD + NEAR_ROWS]
-    near_left = remote(near_out.at[1], near_in.at[1], 9, (ax, left))
-    near_left.start()
+        section[c] += matmul(edges[:, c * LINES : (c + 1) * LINES], place, ((0,), (0,)))
 
     basis = tab("basis")
     for c in range(FIELDS):
@@ -318,6 +345,10 @@
     sign_left = jnp.where(az == 0, -1.0, 1.0)
     sign_right = jnp.where(az == SECTORS - 1, -1.0, 1.0)
     sign_across = jnp.where(az < 2, -1.0, 1.0)
+    self_row = lax.broadcasted_iota(jnp.int32, (2 * NEAR_PAD, FIELDS * LINES), 0)
+    from_edges[MESSAGE_ROWS : MESSAGE_ROWS + 2 * NEAR_PAD] = from_edges[
+        MESSAGE_ROWS : MESSAGE_ROWS + 2 * NEAR_PAD
+    ] * jnp.where(self_row < NEAR_PAD, sign_left, sign_right).astype(jnp.float32)
     signs = jnp.where(part_row < NEAR_PAD, sign_left, jnp.where(part_row < 2 * NEAR_PAD, sign_right, sign_across))
     targets = jnp.concatenate([tab("target_a"), tab("target_b")], axis=1) * signs.astype(jnp.float32)
 
@@ -344,9 +375,10 @@
     far_copy.wait_recv()
     message[2 * NEAR_PAD : 2 * NEAR_PAD + FAR_ROWS] = far_in[...]
     near_right.wait_recv()
-    message[0:NEAR_ROWS] = near_in[0]
+    message[0:NEAR_ROWS] = near_in[0] + from_edges[MESSAGE_ROWS : MESSAGE_ROWS + NEAR_ROWS]
     near_left.wait_recv()
-    message[NEAR_PAD : NEAR_PAD + NEAR_ROWS] = near_in[1]
+    own_left = MESSAGE_ROWS + NEAR_PAD
+    message[NEAR_PAD : NEAR_PAD + NEAR_ROWS] = near_in[1] + from_edges[own_left : own_left + NEAR_ROWS]
     for c in range(FIELDS):
         field = matmul(message[:, c * LINES : (c + 1) * LINES], targets, ((0,), (0,)))
         for x in range(STATIONS):
@@ -361,7 +393,7 @@
 
     pl.when(has_high)(to_high.wait_send)
     pl.when(has_low)(to_low.wait_send)
-    for copy in (edge_left, edge_right, mirror_copy, extra_left, extra_right, far_copy, near_right, near_left):
+    for copy in (edge_left, edge_right, extra_left, extra_right, far_copy, near_right, near_left):
         copy.wait_send()
 
 
@@ -412,10 +444,12 @@
             pltpu.VMEM((FAR_ROWS, lines), f32),
             pltpu.VMEM((FAR_ROWS, lines), f32),
             pltpu.VMEM((MESSAGE_ROWS, lines), f32),
+            pltpu.VMEM((2 * MESSAGE_ROWS, lines), f32),
             pltpu.VMEM((80, WIDTH), f32),
             pltpu.SemaphoreType.DMA((4,)),
             pltpu.SemaphoreType.DMA((10,)),
             pltpu.SemaphoreType.DMA((10,)),
+            pltpu.SemaphoreType.REGULAR,
         ],
         compiler_params=pltpu.CompilerParams(
             collective_id=0, has_side_effects=True, vmem_limit_bytes=60 * 1024 * 1024

time: 67.5 us -> 64 us (0.948)
  the two profiles are of different devices: /device:TPU:46 before, /device:TPU:32 now
where the time goes in v3:
time: 64 us; the launch traced here: 63.8 us
  Pallas kernels  62 us (97%)
  local copies, waits for them, and re-layouts  1.72 us (3%)
    pallas_call x1, Pallas kernels, per_device(): pl.pallas_call(body, out_shape=jax.ShapeDtypeStruct(block, f32), in_specs...  62 us
    unnamed x1, local copies, waits for them, and re-layouts  1.72 us

profile of v3, /device:TPU:32, one launch (start us, length us, event | category | flops | bytes accessed | tf_op | source)
XLA Modules:
  0.0 63.8 jit_solution(11825479162183528073)
XLA Ops:
  0.0 62.0 %shard_map.46 = f32[4,5,32,128]{3,2,1,0:T(8,128)} custom-call(f32[4,5,32,128]{3,2,1,0:T(8,128)} %conserved.1, f32[800,128]{1,0:T(8,128)} %constant.2.clone.tables, s32[32]{0:T(128)} %modes.1, s32[4]{0:T(128)} %counts.1), custom_call_target="tpu_custom_call" | custom-call | tf_op jit(solution)/shard_map/pallas_call | solution.py:412
  62.1 1.7 %copy.6 = f32[4,5,32,128]{3,2,1,0:T(8,128)} copy(f32[4,5,32,128]{3,2,1,0:T(8,128)} %shard_map.46) | data formatting | bytes 655360

commit v4 on v3

--- a/solution.py
+++ b/solution.py
@@ -254,8 +254,8 @@
 
     load_table.wait()
     edges = matmul(tab("edge"), flux_h[...].reshape(FIELDS * LINES, WIDTH), ((1,), (1,)))
-    edge_out[0] = edges[0:4]
-    edge_out[1] = edges[4:8]
+    pack(edge_out, edges[0:4], 0)
+    pack(edge_out, edges[4:8], 1)
     edge_waves = jnp.concatenate(
         [edges * jnp.concatenate([edge_c] * FIELDS, axis=1), edges * jnp.concatenate([edge_s] * FIELDS, axis=1)], axis=0
     )
@@ -271,7 +271,8 @@
     mirror_mod[80:128] = jnp.zeros((48, 2 * WIDTH), jnp.float32)
     sources = jnp.concatenate([tab("source_a"), tab("source_b")], axis=1)
     extra = matmul(sources, mirror_mod[...], ((1,), (1,)))
-    extra_out[...] = extra[0 : 2 * NEAR_PAD]
+    extra_out[0] = extra[0:NEAR_ROWS]
+    extra_out[1] = extra[NEAR_PAD : NEAR_PAD + NEAR_ROWS]
     extra_own[...] = extra[2 * NEAR_PAD : 64]
     radial_table = tab("radial")
     swirl_table = tab("swirl")
@@ -289,12 +290,10 @@
     to_low = remote(axial_out.at[0], axial_in.at[1], 1, (ax - 1, az))
     edge_left = remote(edge_out.at[0], edge_in.at[0], 2, (ax, left))
     edge_right = remote(edge_out.at[1], edge_in.at[1], 3, (ax, right))
-    extra_left = remote(extra_out.at[0:NEAR_PAD], extra_in.at[0:NEAR_PAD], 5, (ax, left))
-    extra_right = remote(
-        extra_out.at[NEAR_PAD : 2 * NEAR_PAD], extra_in.at[NEAR_PAD : 2 * NEAR_PAD], 6, (ax, right)
-    )
+    extra_left = remote(extra_out.at[0], extra_in.at[0], 5, (ax, left))
+    extra_right = remote(extra_out.at[1], extra_in.at[1], 6, (ax, right))
     mirror_copy = remote(mirror_out, mirror_in, 4, (ax, across))
-    far_copy = remote(far_out, far_in, 7, (ax, across))
+    far_copy = remote(far_out.at[0], far_in.at[0], 7, (ax, across))
     near_right = remote(near_out.at[0], near_in.at[0], 8, (ax, right))
     near_left = remote(near_out.at[1], near_in.at[1], 9, (ax, left))
     for sector in (right, left):
@@ -318,9 +317,9 @@
             modulated[pl.ds(c * LINES + x * ROWS, ROWS), 0:WIDTH] = value * wave_c
             modulated[pl.ds(c * LINES + x * ROWS, ROWS), WIDTH : 2 * WIDTH] = value * wave_s
     messages = matmul(sources, modulated[...], ((1,), (1,))) + from_edges[0:MESSAGE_ROWS]
-    far_out[...] = messages[2 * NEAR_PAD : 2 * NEAR_PAD + FAR_ROWS]
-    near_out[0] = messages[0:NEAR_ROWS]
-    near_out[1] = messages[NEAR_PAD : NEAR_PAD + NEAR_ROWS]
+    pack(far_out, messages[2 * NEAR_PAD : 2 * NEAR_PAD + FAR_ROWS], 0)
+    pack(near_out, messages[0:NEAR_ROWS], 0)
+    pack(near_out, messages[NEAR_PAD : NEAR_PAD + NEAR_ROWS], 1)
     far_copy.start()
     mirror_copy.wait_send()
     near_right.start()
@@ -328,7 +327,7 @@
 
     edge_left.wait_recv()
     edge_right.wait_recv()
-    edges = jnp.concatenate([edge_in[0], edge_in[1]], axis=0)
+    edges = jnp.concatenate([unpack(edge_in, 4, 0), unpack(edge_in, 4, 1)], axis=0)
     place = tab("place")
     for c in range(FIELDS):
         section[c] += matmul(edges[:, c * LINES : (c + 1) * LINES], place, ((0,), (0,)))
@@ -354,7 +353,8 @@
 
     extra_left.wait_recv()
     extra_right.wait_recv()
-    extra = jnp.concatenate([extra_in[...], extra_own[...]], axis=0)
+    fill = jnp.zeros((NEAR_PAD - NEAR_ROWS, WIDTH), jnp.float32)
+    extra = jnp.concatenate([extra_in[0], fill, extra_in[1], fill, extra_own[...]], axis=0)
     extra_field = matmul(extra, targets, ((0,), (0,)))
     mirror_copy.wait_recv()
     mirrored = mirror_in[...]
@@ -373,12 +373,12 @@
             compact[lines] = jnp.where((row & 3) < limit, smooth, mirror_in[lines])
 
     far_copy.wait_recv()
-    message[2 * NEAR_PAD : 2 * NEAR_PAD + FAR_ROWS] = far_in[...]
+    message[2 * NEAR_PAD : 2 * NEAR_PAD + FAR_ROWS] = unpack(far_in, FAR_ROWS, 0)
     near_right.wait_recv()
-    message[0:NEAR_ROWS] = near_in[0] + from_edges[MESSAGE_ROWS : MESSAGE_ROWS + NEAR_ROWS]
+    message[0:NEAR_ROWS] = unpack(near_in, NEAR_ROWS, 0) + from_edges[MESSAGE_ROWS : MESSAGE_ROWS + NEAR_ROWS]
     near_left.wait_recv()
     own_left = MESSAGE_ROWS + NEAR_PAD
-    message[NEAR_PAD : NEAR_PAD + NEAR_ROWS] = near_in[1] + from_edges[own_left : own_left + NEAR_ROWS]
+    message[NEAR_PAD : NEAR_PAD + NEAR_ROWS] = unpack(near_in, NEAR_ROWS, 1) + from_edges[own_left : own_left + NEAR_ROWS]
     for c in range(FIELDS):
         field = matmul(message[:, c * LINES : (c + 1) * LINES], targets, ((0,), (0,)))
         for x in range(STATIONS):
@@ -395,6 +395,16 @@
     pl.when(has_low)(to_low.wait_send)
     for copy in (edge_left, edge_right, extra_left, extra_right, far_copy, near_right, near_left):
         copy.wait_send()
+
+
+def pack(ref, value, slot):
+    rows = value.shape[0]
+    for c in range(FIELDS):
+        ref[slot, c * rows : (c + 1) * rows] = value[:, c * LINES : (c + 1) * LINES]
+
+
+def unpack(ref, rows, slot):
+    return jnp.concatenate([ref[slot, c * rows : (c + 1) * rows] for c in range(FIELDS)], axis=1)
 
 
 def store(ref, index, value):
@@ -429,20 +439,20 @@
             pltpu.VMEM((FIELDS, LINES, WIDTH), f32),
             pltpu.VMEM((2,) + block, f32),
             pltpu.VMEM((2,) + block, f32),
-            pltpu.VMEM((2, 4, lines), f32),
-            pltpu.VMEM((2, 4, lines), f32),
+            pltpu.VMEM((2, FIELDS * 4, LINES), f32),
+            pltpu.VMEM((2, FIELDS * 4, LINES), f32),
             pltpu.VMEM((80, WIDTH), f32),
             pltpu.VMEM((80, WIDTH), f32),
             pltpu.VMEM((128, 2 * WIDTH), f32),
-            pltpu.VMEM((2 * NEAR_PAD, WIDTH), f32),
-            pltpu.VMEM((2 * NEAR_PAD, WIDTH), f32),
+            pltpu.VMEM((2, NEAR_ROWS, WIDTH), f32),
+            pltpu.VMEM((2, NEAR_ROWS, WIDTH), f32),
             pltpu.VMEM((16, WIDTH), f32),
             pltpu.VMEM((FIELDS, LINES, WIDTH), f32),
             pltpu.VMEM((lines, 2 * WIDTH), f32),
-            pltpu.VMEM((2, NEAR_ROWS, lines), f32),
-            pltpu.VMEM((2, NEAR_ROWS, lines), f32),
-            pltpu.VMEM((FAR_ROWS, lines), f32),
-            pltpu.VMEM((FAR_ROWS, lines), f32),
+            pltpu.VMEM((2, FIELDS * NEAR_ROWS, LINES), f32),
+            pltpu.VMEM((2, FIELDS * NEAR_ROWS, LINES), f32),
+            pltpu.VMEM((1, FIELDS * FAR_ROWS, LINES), f32),
+            pltpu.VMEM((1, FIELDS * FAR_ROWS, LINES), f32),
             pltpu.VMEM((MESSAGE_ROWS, lines), f32),
             pltpu.VMEM((2 * MESSAGE_ROWS, lines), f32),
             pltpu.VMEM((80, WIDTH), f32),

time: 64 us -> 60.7 us (0.948)
  the two profiles are of different devices: /device:TPU:32 before, /device:TPU:127 now
where the time goes in v4:
time: 60.7 us; the launch traced here: 60.5 us
  Pallas kernels  58.8 us (97%)
  local copies, waits for them, and re-layouts  1.72 us (3%)
    pallas_call x1, Pallas kernels, per_device(): pl.pallas_call(body, out_shape=jax.ShapeDtypeStruct(block, f32), in_specs...  58.8 us
    unnamed x1, local copies, waits for them, and re-layouts  1.72 us

profile of v4, /device:TPU:127, one launch (start us, length us, event | category | flops | bytes accessed | tf_op | source)
XLA Modules:
  0.0 60.5 jit_solution(14483104443826235156)
XLA Ops:
  0.0 58.8 %shard_map.46 = f32[4,5,32,128]{3,2,1,0:T(8,128)} custom-call(f32[4,5,32,128]{3,2,1,0:T(8,128)} %conserved.1, f32[800,128]{1,0:T(8,128)} %constant.2.clone.tables, s32[32]{0:T(128)} %modes.1, s32[4]{0:T(128)} %counts.1), custom_call_target="tpu_custom_call" | custom-call | tf_op jit(solution)/shard_map/pallas_call | solution.py:422
  58.8 1.7 %copy.6 = f32[4,5,32,128]{3,2,1,0:T(8,128)} copy(f32[4,5,32,128]{3,2,1,0:T(8,128)} %shard_map.46) | data formatting | bytes 655360

commit v5 on v4

--- a/solution.py
+++ b/solution.py
@@ -298,10 +298,10 @@
     near_left = remote(near_out.at[1], near_in.at[1], 9, (ax, left))
     for sector in (right, left):
         pl.semaphore_signal(go_sem, inc=1, device_id=(ax, sector), device_id_type=MESH)
+    pl.when(has_high)(to_high.start)
+    pl.when(has_low)(to_low.start)
     edge_left.start()
     edge_right.start()
-    pl.when(has_high)(to_high.start)
-    pl.when(has_low)(to_low.start)
     extra_left.start()
     extra_right.start()
     pl.semaphore_wait(go_sem, 2)

time: 60.7 us -> 60.8 us (level)
  the two profiles are of different devices: /device:TPU:127 before, /device:TPU:32 now
where the time goes in v5:
time: 60.8 us; the launch traced here: 60.6 us
  Pallas kernels  58.9 us (97%)
  local copies, waits for them, and re-layouts  1.72 us (3%)
    pallas_call x1, Pallas kernels, per_device(): pl.pallas_call(body, out_shape=jax.ShapeDtypeStruct(block, f32), in_specs...  58.9 us
    unnamed x1, local copies, waits for them, and re-layouts  1.72 us

profile of v5, /device:TPU:32, one launch (start us, length us, event | category | flops | bytes accessed | tf_op | source)
XLA Modules:
  0.0 60.6 jit_solution(9245207536299536444)
XLA Ops:
  0.0 58.9 %shard_map.46 = f32[4,5,32,128]{3,2,1,0:T(8,128)} custom-call(f32[4,5,32,128]{3,2,1,0:T(8,128)} %conserved.1, f32[800,128]{1,0:T(8,128)} %constant.2.clone.tables, s32[32]{0:T(128)} %modes.1, s32[4]{0:T(128)} %counts.1), custom_call_target="tpu_custom_call" | custom-call | tf_op jit(solution)/shard_map/pallas_call | solution.py:422
  58.9 1.7 %copy.6 = f32[4,5,32,128]{3,2,1,0:T(8,128)} copy(f32[4,5,32,128]{3,2,1,0:T(8,128)} %shard_map.46) | data formatting | bytes 655360
